TPU v7x, 32 devices: a whole 2x2x4 slice. The times are simulated.
32 devices in a mesh: wide: 16 (over z, y, core), narrow: 2 (over x).
Axes of the slice: x: 2, y: 2, z: 4, core: 2. Of those that a mesh axis runs over, the one named last changes fastest.
Arguments:
- tokens: bfloat16 [128, 128, 768], P(('wide', 'narrow')), may hold values from -6 to 6
- land_mask: int32 [128, 128], P(('wide', 'narrow')), may hold values from 0 to 1, as said below
- cotangent: bfloat16 [128, 128, 768], P(('wide', 'narrow')), may hold values from -6 to 6
- qkv_weight: bfloat16 [768, 2304], replicated, may hold values from -0.21875 to 0.21875
- query_bias: float32 [768], replicated, may hold values from -3 to 3
- value_bias: float32 [768], replicated, may hold values from -3 to 3
- proj_weight: bfloat16 [768, 768], replicated, may hold values from -0.625 to 0.625
- proj_bias: float32 [768], replicated, may hold values from -3 to 3
- up_weight: bfloat16 [768, 3072], replicated, may hold values from -0.21875 to 0.21875
- up_bias: float32 [3072], replicated, may hold values from -3 to 3
- down_weight: bfloat16 [3072, 768], replicated, may hold values from -0.109375 to 0.109375
- down_bias: float32 [768], replicated, may hold values from -3 to 3
- norm1_gain: float32 [768], replicated, may hold values from 0.1 to 1.9
- norm1_shift: float32 [768], replicated, may hold values from -2 to 2
- norm2_gain: float32 [768], replicated, may hold values from 0.1 to 1.9
- norm2_shift: float32 [768], replicated, may hold values from -2 to 2
Outputs:
- output: bfloat16 [128, 128, 768], P(('wide', 'narrow'))
- tokens_grad: float32 [128, 128, 768], P(('wide', 'narrow'))
- qkv_grad: float32 [768, 2304], P('wide', 'narrow')
- query_bias_grad: float32 [768], replicated
- value_bias_grad: float32 [768], replicated
- proj_grad: float32 [768, 768], P('wide', 'narrow')
- proj_bias_grad: float32 [768], replicated
- up_grad: float32 [768, 3072], P('wide', 'narrow')
- up_bias_grad: float32 [3072], replicated
- down_grad: float32 [3072, 768], P('wide', 'narrow')
- down_bias_grad: float32 [768], replicated
- norm1_gain_grad: float32 [768], replicated
- norm1_shift_grad: float32 [768], replicated
- norm2_gain_grad: float32 [768], replicated
- norm2_shift_grad: float32 [768], replicated
Inputs may be any that keep to these rules, and one draw needn't show every extreme that they name: `land_mask`: every field holds at least one land patch; in every draw one field is all land and another holds a single land patch; which slots are land is random.
All inputs are finite; a program needn't handle non-finite values.
Results may differ from a plain program's by a relative error of at most 0.012.
Values sent between devices are 32-bit elements; how exact they have to be, the bound alone decides.
A program may use at most 192 MiB of HBM per device.

v0:
```python
import jax
import jax.numpy as jnp
from jax import lax
from jax.sharding import PartitionSpec as P

HEADS = 12


def layer_norm(inputs, norm_gain, norm_shift):
    average = jnp.mean(inputs, -1, keepdims=True)
    centred = inputs - average
    variance = jnp.mean(centred * centred, -1, keepdims=True)
    return centred * lax.rsqrt(variance + 1e-06) * norm_gain + norm_shift


def attend_scores(queries, key_rows, visible, scaling):
    scores = (
        jnp.einsum("fqhe,fkhe->fhqk", queries, key_rows, preferred_element_type=jnp.float32)
        * scaling
    )
    return jnp.where(visible[:, None, None, :], scores, -1e30)


def share_sums(former, latter):
    row_sums = (
        lax.psum_scatter(former, "wide", scatter_dimension=0, tiled=True),
        lax.psum_scatter(latter, "wide", scatter_dimension=0, tiled=True),
    )
    return (
        lax.psum_scatter(row_sums[0], "narrow", scatter_dimension=1, tiled=True),
        lax.psum_scatter(row_sums[1], "narrow", scatter_dimension=1, tiled=True),
    )


def local(
    tokens,
    land_mask,
    cotangent,
    qkv_weight,
    query_bias,
    value_bias,
    proj_weight,
    proj_bias,
    up_weight,
    up_bias,
    down_weight,
    down_bias,
    norm1_gain,
    norm1_shift,
    norm2_gain,
    norm2_shift,
):
    field_count, length, model_width = tokens.shape
    head_count = HEADS
    head_width = model_width // head_count
    scaling = head_width ** (-0.5)
    visible = land_mask > 0
    split_shape = (field_count, length, head_count, head_width)
    source = tokens.astype(jnp.float32)
    normed_one = layer_norm(source, norm1_gain, norm1_shift).astype(jnp.bfloat16)
    joint = jnp.einsum("fpd,de->fpe", normed_one, qkv_weight, preferred_element_type=jnp.float32)
    queries = (joint[..., :model_width] + query_bias).astype(jnp.bfloat16).reshape(split_shape)
    key_rows = joint[..., model_width : 2 * model_width].astype(jnp.bfloat16).reshape(split_shape)
    values = (joint[..., 2 * model_width :] + value_bias).astype(jnp.bfloat16).reshape(split_shape)
    scores = attend_scores(queries, key_rows, visible, scaling)
    highest = jnp.max(scores, -1, keepdims=True)
    exponent = jnp.exp(scores - highest)
    summed = jnp.sum(exponent, -1, keepdims=True)
    attention = exponent / summed
    log_total = highest + jnp.log(summed)
    attended = jnp.einsum(
        "fhqk,fkhe->fqhe",
        attention.astype(jnp.bfloat16),
        values,
        preferred_element_type=jnp.float32,
    )
    attended = attended.reshape(field_count, length, model_width).astype(jnp.bfloat16)
    middle = (
        source
        + jnp.einsum("fpd,de->fpe", attended, proj_weight, preferred_element_type=jnp.float32)
        + proj_bias
    )
    normed_two = layer_norm(middle, norm2_gain, norm2_shift).astype(jnp.bfloat16)
    hidden = (
        jnp.einsum("fpd,dn->fpn", normed_two, up_weight, preferred_element_type=jnp.float32)
        + up_bias
    )
    activated_full, gelu_pull = jax.vjp(jax.nn.gelu, hidden)
    activated = activated_full.astype(jnp.bfloat16)
    output = (
        middle
        + jnp.einsum("fpn,nd->fpd", activated, down_weight, preferred_element_type=jnp.float32)
        + down_bias
    )
    grad_out = cotangent.astype(jnp.float32)
    down_local = jnp.einsum("fpn,fpd->nd", activated, cotangent, preferred_element_type=jnp.float32)
    down_bias_local = jnp.sum(grad_out, axis=(0, 1))
    activated_grad = jnp.einsum(
        "fpd,nd->fpn", cotangent, down_weight, preferred_element_type=jnp.float32
    )
    hidden_grad = gelu_pull(activated_grad)[0].astype(jnp.bfloat16)
    up_local = jnp.einsum(
        "fpd,fpn->dn", normed_two, hidden_grad, preferred_element_type=jnp.float32
    )
    up_bias_local = jnp.sum(hidden_grad.astype(jnp.float32), axis=(0, 1))
    feed_sums = share_sums(up_local, down_local)
    normed_two_grad = jnp.einsum(
        "fpn,dn->fpd", hidden_grad, up_weight, preferred_element_type=jnp.float32
    )
    unused_two, norm_two_pull = jax.vjp(layer_norm, middle, norm2_gain, norm2_shift)
    middle_part, gain_two_local, shift_two_local = norm_two_pull(normed_two_grad)
    middle_grad = grad_out + middle_part
    middle_low = middle_grad.astype(jnp.bfloat16)
    proj_local = jnp.einsum("fpd,fpe->de", attended, middle_low, preferred_element_type=jnp.float32)
    proj_bias_local = jnp.sum(middle_low.astype(jnp.float32), axis=(0, 1))
    attended_grad = jnp.einsum(
        "fpe,de->fpd", middle_low, proj_weight, preferred_element_type=jnp.float32
    )
    attended_grad = attended_grad.astype(jnp.bfloat16).reshape(split_shape)
    scores = attend_scores(queries, key_rows, visible, scaling)
    attention = jnp.exp(scores - log_total)
    values_grad = jnp.einsum(
        "fhqk,fqhe->fkhe",
        attention.astype(jnp.bfloat16),
        attended_grad,
        preferred_element_type=jnp.float32,
    )
    attention_grad = jnp.einsum(
        "fqhe,fkhe->fhqk", attended_grad, values, preferred_element_type=jnp.float32
    )
    inner_sum = jnp.sum(attention * attention_grad, -1, keepdims=True)
    scores_grad = (attention * (attention_grad - inner_sum)).astype(jnp.bfloat16)
    queries_grad = (
        jnp.einsum("fhqk,fkhe->fqhe", scores_grad, key_rows, preferred_element_type=jnp.float32)
        * scaling
    )
    keys_grad = (
        jnp.einsum("fhqk,fqhe->fkhe", scores_grad, queries, preferred_element_type=jnp.float32)
        * scaling
    )
    flat_shape = (field_count, length, model_width)
    joint_grad = jnp.concatenate(
        [
            queries_grad.reshape(flat_shape),
            keys_grad.reshape(flat_shape),
            values_grad.reshape(flat_shape),
        ],
        -1,
    ).astype(jnp.bfloat16)
    qkv_local = jnp.einsum(
        "fpd,fpe->de", normed_one, joint_grad, preferred_element_type=jnp.float32
    )
    joint_sums = jnp.sum(joint_grad.astype(jnp.float32), axis=(0, 1))
    query_bias_local = joint_sums[:model_width]
    value_bias_local = joint_sums[2 * model_width :]
    attention_sums = share_sums(qkv_local, proj_local)
    normed_one_grad = jnp.einsum(
        "fpe,de->fpd", joint_grad, qkv_weight, preferred_element_type=jnp.float32
    )
    unused_one, norm_one_pull = jax.vjp(layer_norm, source, norm1_gain, norm1_shift)
    source_part, gain_one_local, shift_one_local = norm_one_pull(normed_one_grad)
    tokens_grad = middle_grad + source_part
    vectors = lax.psum(
        (
            query_bias_local,
            value_bias_local,
            proj_bias_local,
            up_bias_local,
            down_bias_local,
            gain_one_local,
            shift_one_local,
            gain_two_local,
            shift_two_local,
        ),
        ("wide", "narrow"),
    )
    return (
        output.astype(jnp.bfloat16),
        tokens_grad,
        attention_sums[0],
        vectors[0],
        vectors[1],
        attention_sums[1],
        vectors[2],
        feed_sums[0],
        vectors[3],
        feed_sums[1],
        vectors[4],
        vectors[5],
        vectors[6],
        vectors[7],
        vectors[8],
    )


def solution(mesh):
    placed = (
        P(("wide", "narrow"), None, None),
        P(("wide", "narrow"), None),
        P(("wide", "narrow"), None, None),
        P(),
        P(),
        P(),
        P(),
        P(),
        P(),
        P(),
        P(),
        P(),
        P(),
        P(),
        P(),
        P(),
    )
    return jax.shard_map(
        local,
        mesh=mesh,
        in_specs=placed,
        out_specs=(
            P(("wide", "narrow"), None, None),
            P(("wide", "narrow"), None, None),
            P("wide", "narrow"),
            P(),
            P(),
            P("wide", "narrow"),
            P(),
            P("wide", "narrow"),
            P(),
            P("wide", "narrow"),
            P(),
            P(),
            P(),
            P(),
            P(),
        ),
        check_vma=False,
    )
```

profile of v0, /device:TPU:0, one launch (start us, length us, event | category | flops | bytes accessed | tf_op | source)
XLA Modules:
  0.0 514.3 jit_solution(11021786195282717744)
XLA Ops:
  7.2 1.5 convert_reduce_fusion.2
  8.7 1.5 fusion.32
  10.8 3.3 fusion.17
  14.1 1.0 slice.33
  15.1 1.4 fusion.37
  16.5 2.3 copy.50
  18.8 2.3 copy.51
  21.1 2.3 copy.52
  23.4 2.4 fusion.59
  25.9 0.7 fusion.19
  26.6 1.0 copy-done.14
  28.3 1.2 copy-done.3
  29.9 0.9 fusion.60
  31.3 2.7 fusion.13
  34.1 7.4 %convert_reduce_fusion = (f32[3072]{0:T(1024)}, bf16[4,128,3072]{2,1,0:T(8,128)(2,1)S(1)}) fusion(f32[4,128,3072]{2,1,0:T(8,128)S(1)} %fusion.13, f32[3072]{0:T(1024)S(1)} %copy-done.35, bf16[4,128,768]{2,1,0:T(8,128)(2,1)S(1)} %copy-done.11, bf16[3072,768]{1,0:T(8,128)(2,1)S(1)} %bitcast.90), kind=kOutput, calls=%fused_computation.9 | convolution fusion | flops 2452091904 | bytes 14966784 | tf_op jit(solution)/shard_map/fpd,nd->fpn/dot_general | solution.py:98
  41.4 3.5 multiply_reduce_fusion.1
  45.7 1.1 copy-done.6
  46.8 0.9 convert_reduce_fusion.4
  47.7 0.9 copy-done.13
  48.6 2.2 convolution_bitcast_fusion.3
  51.0 3.3 convolution_convert_fusion
  54.3 2.3 copy.55
  56.6 0.8 log_add_fusion
  57.4 4.4 fusion.43
  61.8 2.3 copy.61
  64.1 3.6 multiply_reduce_fusion
  67.8 0.9 multiply_convert_fusion.1
  68.7 1.1 copy-done.8
  69.8 2.1 multiply_convert_fusion.2
  71.9 2.3 copy.60
  74.2 3.1 multiply_convert_fusion.3
  77.3 2.3 copy.59
  79.6 7.0 %convolution_bitcast_fusion = f32[768,2304]{1,0:T(8,128)} fusion(bf16[4,128,768]{2,1,0:T(8,128)(2,1)} %param.16, f32[768]{0:T(1024)S(1)} %copy-done.21, f32[768]{0:T(1024)S(1)} %copy-done.19, f32[4,128]{1,0:T(4,128)S(1)} %fusion.53, f32[4,128]{1,0:T(4,128)S(1)} %broadcast_multiply_fusion.1, bf16[4,128,768]{2,1,0:T(8,128)(2,1)} %copy.61, ...), kind=kOutput, calls=%fused_computation.11 | convolution fusion | flops 1821376512 | bytes 10233856 | tf_op jit(solution)/shard_map/fpd,fpe->de/dot_general | solution.py:150
  87.2 8.9 %convolution_bitcast_fusion.2 = f32[768,3072]{1,0:T(8,128)} fusion(bf16[4,128,3072]{2,1,0:T(8,128)(2,1)} %copy-done.38, f32[4,128,768]{2,1,0:T(8,128)} %copy-done.5, f32[768]{0:T(1024)} %param.31, f32[768]{0:T(1024)} %param.30, f32[4,128]{1,0:T(4,128)} %copy-done.29, f32[4,128]{1,0:T(4,128)S(1)} %copy-done.23), kind=kOutput, calls=%fused_computation.13 | convolution fusion | flops 2417885184 | bytes 14166016 | tf_op jit(solution)/shard_map/fpd,fpn->dn/dot_general | solution.py:102
  96.5 10.3 %convolution_bitcast_fusion.1 = f32[3072,768]{1,0:T(8,128)} fusion(bf16[4,128,768]{2,1,0:T(8,128)(2,1)} %param.18, f32[4,128,3072]{2,1,0:T(8,128)} %copy-done.37, f32[3072]{0:T(1024)} %param.25), kind=kOutput, calls=%fused_computation.12 | convolution fusion | flops 2431647744 | bytes 16527360 | tf_op jit(solution)/shard_map/fpn,fpd->nd/dot_general | solution.py:96
  106.9 9.7 %reduce-scatter.13.cloned.1.call-done = f32[48,768]{1,0:T(8,128)} async-done(((f32[768,768]{1,0:T(8,128)}), f32[48,768]{1,0:T(8,128)}) %reduce-scatter.13.cloned.1.call-update) | async-done | bytes 147472 | tf_op jit(solution)/shard_map/reduce_scatter | solution.py:27
  116.6 93.6 %reduce-scatter.9.cloned.1.call-done = f32[48,2304]{1,0:T(8,128)} async-done(((f32[768,2304]{1,0:T(8,128)}), f32[48,2304]{1,0:T(8,128)}) %reduce-scatter.9.cloned.1.call-update) | async-done | bytes 442384 | tf_op jit(solution)/shard_map/reduce_scatter | solution.py:26
  210.3 5.6 %fusion.55 = (f32[768]{0:T(1024)}, f32[4,128]{1,0:T(4,128)}, f32[4,128,768]{2,1,0:T(8,128)}) fusion(f32[768]{0:T(1024)S(1)} %copy-done.19, f32[4,128]{1,0:T(4,128)S(1)} %broadcast_multiply_fusion.1, bf16[4,128,768]{2,1,0:T(8,128)(2,1)} %param.16, bf16[768,2304]{1,0:T(8,128)(2,1)S(1)} %copy-done, bf16[4,128,768]{2,1,0:T(8,128)(2,1)} %copy.61, ...), kind=kOutput, calls=%fused_computation.92 | convolution fusion | flops 1821375232 | bytes 8267776 | tf_op jit(solution)/shard_map/fpe,de->fpd/dot_general | solution.py:157
  215.9 109.4 %reduce-scatter.17.cloned.1.call-done = f32[48,3072]{1,0:T(8,128)} async-done(((f32[768,3072]{1,0:T(8,128)}), f32[48,3072]{1,0:T(8,128)}) %reduce-scatter.17.cloned.1.call-update) | async-done | bytes 589840 | tf_op jit(solution)/shard_map/reduce_scatter | solution.py:26
  325.4 2.8 convert_reduce_fusion.1
  328.2 0.7 multiply_multiply_fusion.2
  328.9 2.8 fusion.31
  331.7 2.5 convert_reduce_fusion.3
  334.2 106.7 %reduce-scatter.21.cloned.1.call-done = f32[192,768]{1,0:T(8,128)} async-done(((f32[3072,768]{1,0:T(8,128)}), f32[192,768]{1,0:T(8,128)}) %reduce-scatter.21.cloned.1.call-update) | async-done | bytes 589840 | tf_op jit(solution)/shard_map/reduce_scatter | solution.py:27
  441.0 0.7 fusion.58
  441.7 42.0 %all-reduce = (f32[768]{0:T(1024)}, f32[768]{0:T(1024)}, f32[768]{0:T(1024)}, f32[3072]{0:T(1024)}, f32[768]{0:T(1024)}, /*index=5*/f32[768]{0:T(1024)}, f32[768]{0:T(1024)}, f32[768]{0:T(1024)}, f32[768]{0:T(1024)}) all-reduce(f32[768]{0:T(1024)S(1)} %get-tuple-element.40, ...), channel_id=1, replica_groups=mesh['wide'=16,'narrow'=2] {'wide','narrow'}, use_global_device_ids=true, to_apply=%region_14.15 | all-reduce | flops 9216 | bytes 73728 | tf_op jit(solution)/shard_map/psum | solution.py:163
  483.6 9.5 %add_convert_fusion = bf16[4,128,768]{2,1,0:T(8,128)(2,1)} fusion(f32[4,128,768]{2,1,0:T(8,128)} %copy-done.5, bf16[3072,768]{1,0:T(8,128)(2,1)} %param.26, f32[768]{0:T(1024)} %param.27, f32[4,128,3072]{2,1,0:T(8,128)} %copy-done.37, f32[3072]{0:T(1024)} %param.25), kind=kOutput, calls=%fused_computation.69 | convolution fusion | flops 2432827392 | bytes 13384704 | tf_op jit(solution)/shard_map/fpn,nd->fpd/dot_general | solution.py:92
  493.2 13.8 %reduce-scatter.23.cloned.1.call-done = f32[192,384]{1,0:T(8,128)} async-done(((f32[192,768]{1,0:T(8,128)}), f32[192,384]{1,0:T(8,128)}) %reduce-scatter.23.cloned.1.call-update) | async-done | bytes 294928 | tf_op jit(solution)/shard_map/reduce_scatter | solution.py:31
  (113 shorter events, 4.3 us)
Async XLA Ops:
  7.2 3.6 copy-start
  7.2 109.4 %reduce-scatter.13.cloned.1.call-start = ((), (), s32[]{:S(2)}) async-start(), calls=%async_computation.10 | async-start | bytes 2506752 | tf_op jit(solution)/shard_map/reduce_scatter | solution.py:27
  10.8 4.3 copy-start.30
  10.8 4.3 copy-start.31
  16.5 6.9 %copy-start.34 = (s32[4,128]{1,0:T(4,128)S(1)}, s32[4,128]{1,0:T(4,128)}, u32[]{:S(2)}) copy-start(s32[4,128]{1,0:T(4,128)} %param.17) | copy-start | bytes 6148
  25.8 2.4 copy-start.1
  25.8 2.4 copy-start.18
  25.9 1.7 copy-start.14
  25.9 5.3 %slice-start = ((s8[4718592]{0:T(1024)(128)(4,1)}), s8[4194304]{0:T(1024)(128)(4,1)S(1)}, s32[]{:S(2)}) async-start(s8[4718592]{0:T(1024)(128)(4,1)} %bitcast.87), calls=%async_computation.16 | async-start | bytes 8388608
  26.6 1.6 copy-start.20
  27.6 1.9 copy-start.3
  27.6 2.3 copy-start.15
  27.6 2.3 copy-start.32
  27.6 3.6 slice-start.1
  29.9 1.3 copy-start.33
  29.9 1.3 copy-start.36
  30.8 14.1 %copy-start.5 = (f32[4,128,768]{2,1,0:T(8,128)}, f32[4,128,768]{2,1,0:T(8,128)S(1)}, u32[]{:S(2)}) copy-start(f32[4,128,768]{2,1,0:T(8,128)S(1)} %get-tuple-element.44) | copy-start | bytes 4718596
  30.8 14.1 %copy-start.22 = (f32[4,128]{1,0:T(4,128)}, f32[4,128]{1,0:T(4,128)S(1)}, u32[]{:S(2)}) copy-start(f32[4,128]{1,0:T(4,128)S(1)} %broadcast_multiply_fusion) | copy-start | bytes 6148
  30.9 3.2 slice-start.2
  31.2 13.8 %copy-start.29 = (f32[4,128]{1,0:T(4,128)}, f32[4,128]{1,0:T(4,128)S(1)}, u32[]{:S(2)}) copy-start(f32[4,128]{1,0:T(4,128)S(1)} %fusion.54) | copy-start | bytes 6148
  31.2 2.8 copy-start.11
  31.3 2.8 slice-start.3
  31.3 2.8 copy-start.35
  34.1 7.4 %copy-start.37 = (f32[4,128,3072]{2,1,0:T(8,128)}, f32[4,128,3072]{2,1,0:T(8,128)S(1)}, u32[]{:S(2)}) copy-start(f32[4,128,3072]{2,1,0:T(8,128)S(1)} %fusion.13) | copy-start | bytes 18874372
  41.4 3.5 copy-start.38
  45.6 1.2 copy-start.6
  45.6 2.1 copy-start.26
  50.8 159.5 %reduce-scatter.9.cloned.1.call-start = ((), (), s32[]{:S(2)}) async-start(), calls=%async_computation.8 | async-start | bytes 7520256 | tf_op jit(solution)/shard_map/reduce_scatter | solution.py:26
  57.4 4.4 copy-start.16
  64.1 3.6 copy-start.2
  64.1 3.6 copy-start.17
  67.8 2.1 copy-start.9
  68.7 1.1 copy-start.8
  74.2 5.4 %copy-start.19 = (f32[768]{0:T(1024)S(1)}, f32[768]{0:T(1024)}, u32[]{:S(2)}) copy-start(f32[768]{0:T(1024)} %param.28) | copy-start | bytes 9220
  74.2 5.4 %copy-start.21 = (f32[768]{0:T(1024)S(1)}, f32[768]{0:T(1024)}, u32[]{:S(2)}) copy-start(f32[768]{0:T(1024)} %param.29) | copy-start | bytes 9220
  86.6 238.7 %reduce-scatter.17.cloned.1.call-start = ((), (), s32[]{:S(2)}) async-start(), calls=%async_computation.12 | async-start | bytes 10027008 | tf_op jit(solution)/shard_map/reduce_scatter | solution.py:26
  96.2 344.7 %reduce-scatter.21.cloned.1.call-start = ((), (), s32[]{:S(2)}) async-start(), calls=%async_computation.14 | async-start | bytes 10027008 | tf_op jit(solution)/shard_map/reduce_scatter | solution.py:27
  106.8 386.4 %reduce-scatter.15.cloned.1.call-start = ((), (), s32[]{:S(2)}) async-start(), calls=%async_computation.11 | async-start | bytes 221184 | tf_op jit(solution)/shard_map/reduce_scatter | solution.py:31
  116.6 376.6 %reduce-scatter.11.cloned.1.call-start = ((), (), s32[]{:S(2)}) async-start(), calls=%async_computation.9 | async-start | bytes 663552 | tf_op jit(solution)/shard_map/reduce_scatter | solution.py:30
  210.3 282.9 %reduce-scatter.19.cloned.1.call-start = ((), (), s32[]{:S(2)}) async-start(), calls=%async_computation.13 | async-start | bytes 884736 | tf_op jit(solution)/shard_map/reduce_scatter | solution.py:30
  215.9 112.3 %copy-start.25 = (f32[4,128]{1,0:T(4,128)S(1)}, f32[4,128]{1,0:T(4,128)}, u32[]{:S(2)}) copy-start(f32[4,128]{1,0:T(4,128)} %copy-done.24) | copy-start | bytes 6148
  325.3 181.7 %reduce-scatter.23.cloned.1.call-start = ((), (), s32[]{:S(2)}) async-start(), calls=%async_computation.15 | async-start | bytes 884736 | tf_op jit(solution)/shard_map/reduce_scatter | solution.py:31
  325.3 3.5 copy-start.4
  325.4 6.3 %copy-start.7 = (f32[4,128,768]{2,1,0:T(8,128)S(1)}, f32[4,128,768]{2,1,0:T(8,128)}, u32[]{:S(2)}) copy-start(f32[4,128,768]{2,1,0:T(8,128)} %copy-done.6) | copy-start | bytes 4718596
  325.4 6.3 %copy-start.10 = (f32[4,128,768]{2,1,0:T(8,128)S(1)}, f32[4,128,768]{2,1,0:T(8,128)}, u32[]{:S(2)}) copy-start(f32[4,128,768]{2,1,0:T(8,128)} %get-tuple-element.48) | copy-start | bytes 4718596
  325.4 6.3 %copy-start.12 = (bf16[4,128,768]{2,1,0:T(8,128)(2,1)S(1)}, bf16[4,128,768]{2,1,0:T(8,128)(2,1)}, u32[]{:S(2)}) copy-start(bf16[4,128,768]{2,1,0:T(8,128)(2,1)} %param.18) | copy-start | bytes 2359300
  325.4 6.3 %copy-start.27 = (f32[4,128]{1,0:T(4,128)S(1)}, f32[4,128]{1,0:T(4,128)}, u32[]{:S(2)}) copy-start(f32[4,128]{1,0:T(4,128)} %copy-done.26) | copy-start | bytes 6148
  331.7 110.0 %copy-start.28 = (f32[768]{0:T(1024)S(1)}, f32[768]{0:T(1024)}, u32[]{:S(2)}) copy-start(f32[768]{0:T(1024)} %get-tuple-element.31) | copy-start | bytes 9220
  (3 other events, 2.1 us)
Sparse Core Ops, SparseCore 0:
  50.9 65.6 reduce-scatter.12
  121.1 89.0 reduce-scatter.8
  214.3 110.8 reduce-scatter.16
  329.8 111.1 reduce-scatter.20
  443.6 10.2 reduce-scatter.14
  456.5 13.7 reduce-scatter.10
  473.3 15.6 reduce-scatter.18
  491.8 15.1 reduce-scatter.22
where the time goes:
time: 522 us; the launch traced here: 514 us
  waiting for transfers between devices  333 us (64%)
  matrix products  80.8 us (15%)
  blocking collectives  42 us (8%)
  local copies, waits for them, and re-layouts  24.9 us (5%)
  other arithmetic  17.4 us (3%)
  between operations  15.1 us (3%)
    reduce_scatter x2, waiting for transfers between devices, share_sums(): lax.psum_scatter(former, 'wide', scatter_dimension=0, tiled=True)  203 us
    reduce_scatter x2, waiting for transfers between devices, share_sums(): lax.psum_scatter(latter, 'wide', scatter_dimension=0, tiled=True)  116 us
    psum x1, blocking collectives, local(): lax.psum((query_bias_local, value_bias_local, proj_bias_local, up_bias_lo...  42 us
    reduce_scatter x2, waiting for transfers between devices, share_sums(): lax.psum_scatter(row_sums[1], 'narrow', scatter_dimension=1, tiled=True)  13.8 us
  transfers between devices with their start and end apart: 8, of which 5 were waited for; matrix products, arithmetic and copies ran while one was open for 15% of the time, Pallas kernels for 0%

commit v1 on v0

--- a/solution.py
+++ b/solution.py
@@ -1,9 +1,650 @@
 import jax
 import jax.numpy as jnp
 from jax import lax
+from jax.experimental import pallas as pl
+from jax.experimental.pallas import tpu as pltpu
 from jax.sharding import PartitionSpec as P
 
 HEADS = 12
+F32 = jnp.float32
+BF16 = jnp.bfloat16
+SLOTS = 6
+
+
+def dot(a, b):
+    return lax.dot_general(a, b, (((1,), (0,)), ((), ())), preferred_element_type=F32)
+
+
+def dot_nt(a, b):
+    return lax.dot_general(a, b, (((1,), (1,)), ((), ())), preferred_element_type=F32)
+
+
+def dot_tn(a, b):
+    return lax.dot_general(a, b, (((0,), (0,)), ((), ())), preferred_element_type=F32)
+
+
+def standardise(rows):
+    centred = rows - jnp.mean(rows, -1, keepdims=True)
+    scale = lax.rsqrt(jnp.mean(centred * centred, -1, keepdims=True) + 1e-06)
+    return centred * scale, scale
+
+
+def norm_back(unit_rows, scale, pulled):
+    return scale * (
+        pulled
+        - jnp.mean(pulled, -1, keepdims=True)
+        - unit_rows * jnp.mean(pulled * unit_rows, -1, keepdims=True)
+    )
+
+
+def column_sums(rows):
+    return jnp.sum(rows, axis=0, keepdims=True)
+
+
+def layer_kernel(wide, narrow, fields, patches, *refs):
+    (
+        tokens_in, cotangent_in, qkv_in, proj_in, up_in, down_in,
+        land, query_bias, value_bias, proj_bias, up_bias, down_bias,
+        gain_one, shift_one, gain_two, shift_two,
+        output_out, tokens_out, qkv_out, proj_out, up_out, down_out, vec_out,
+        tok, cot, n1, qkv, att, mid, n2, act_t, act, hgr, acc, ngr, left, w_a, w_b, w_p, qkv_bias,
+        keep, core_in, in_0, in_1, in_2, in_3, vec, vec_in,
+        load_sem, core_send, core_recv, core_free, stage_send, stage_recv, final_sem,
+        vec_send, vec_recv, store_sem,
+    ) = refs
+    model = tok.shape[1]
+    hidden_width = w_a.shape[1]
+    stage_in = (in_0, in_1, in_2, in_3)
+    at_wide = lax.axis_index("wide")
+    at_narrow = lax.axis_index("narrow")
+    width = model // narrow
+    block_rows = model // wide
+    group_rows = block_rows // 3
+    chunk = width
+
+    def my_bit(axis, level):
+        index = at_wide if axis == "wide" else at_narrow
+        return lax.rem(lax.div(index, 1 << level), 2)
+
+    def partner(axis, level):
+        shift = (1 << level) * (1 - 2 * my_bit(axis, level))
+        if axis == "wide":
+            return (at_wide + shift, at_narrow)
+        return (at_wide, at_narrow + shift)
+
+    wide_bits = [("wide", i) for i in range(1, wide.bit_length() - 1)]
+    narrow_bits = [("narrow", i) for i in range(narrow.bit_length() - 1)]
+    all_bits = [("wide", 0)] + wide_bits + narrow_bits
+    stages = len(wide_bits) + len(narrow_bits)
+    blocks = 1 << stages
+    core = my_bit("wide", 0)
+    mine = {bit: my_bit(*bit) for bit in all_bits}
+    to = {bit: partner(*bit) for bit in all_bits}
+
+    def order(unit, group):
+        if group == 0:
+            return narrow_bits + wide_bits
+        if group == 1:
+            return wide_bits[:1] + narrow_bits + wide_bits[1:]
+        if unit % 2 == 0:
+            return wide_bits[1:2] + narrow_bits + wide_bits[:1] + wide_bits[2:]
+        return wide_bits[1:2] + wide_bits[:1] + narrow_bits + wide_bits[2:]
+
+    def place(unit, group, row_block, column_block):
+        found = 0
+        for axis, level in order(unit, group):
+            index = row_block if axis == "wide" else column_block
+            found = 2 * found + ((index >> level) & 1)
+        return found
+
+    barrier = pltpu.get_barrier_semaphore()
+    for bit in all_bits:
+        pl.semaphore_signal(
+            barrier, inc=1, device_id=to[bit], device_id_type=pl.DeviceIdType.MESH
+        )
+
+    def remote(src, dst, send, recv, bit):
+        return pltpu.make_async_remote_copy(
+            src_ref=src, dst_ref=dst, send_sem=send, recv_sem=recv,
+            device_id=to[bit], device_id_type=pl.DeviceIdType.MESH,
+        )
+
+    def core_copy(unit):
+        slot = unit % 2
+        return remote(
+            keep.at[SLOTS + slot], core_in.at[slot],
+            core_send.at[slot], core_recv.at[slot], ("wide", 0),
+        )
+
+    def core_start(unit):
+        if unit >= 2:
+            pl.semaphore_wait(core_free, 1)
+        core_copy(unit).start()
+
+    def span(unit, group, stage):
+        half = blocks >> (stage + 1)
+        sequence = order(unit, group)
+        base = 0
+        for earlier in range(stage):
+            base = base + mine[sequence[earlier]] * (blocks >> (earlier + 1))
+        bit = sequence[stage]
+        return half, base + mine[bit] * half, base + (1 - mine[bit]) * half, bit
+
+    def stage_copy(unit, group, stage):
+        half, own, other, bit = span(unit, group, stage)
+        return remote(
+            keep.at[unit % SLOTS, group, pl.ds(other, half)],
+            stage_in[stage].at[unit, group],
+            stage_send.at[unit, stage, group],
+            stage_recv.at[unit, stage, group],
+            bit,
+        )
+
+    def core_end(unit):
+        slot = unit % 2
+        core_copy(unit).wait()
+
+        def step(block, carry):
+            for group in range(3):
+                keep[unit % SLOTS, group, block] += core_in[slot, group, block]
+            return carry
+
+        lax.fori_loop(0, blocks, step, 0)
+        if unit + 2 < 12:
+            pl.semaphore_signal(
+                core_free, inc=1, device_id=to[("wide", 0)],
+                device_id_type=pl.DeviceIdType.MESH,
+            )
+        for group in range(3):
+            stage_copy(unit, group, 0).start()
+
+    def final_copy(unit, group):
+        half, own, other, bit = span(unit, group, stages - 1)
+        ref, row, column = (
+            (up_out, 0, unit * width),
+            (down_out, (unit - 4) * block_rows, 0),
+            (proj_out, 0, 0),
+            (qkv_out, 0, (unit - 9) * width),
+        )[0 if unit < 4 else 1 if unit < 8 else 2 if unit == 8 else 3]
+        return pltpu.make_async_copy(
+            keep.at[unit % SLOTS, group, own],
+            ref.at[pl.ds(row + group * group_rows, group_rows), pl.ds(column, width)],
+            final_sem.at[unit % SLOTS, group],
+        )
+
+    def stage_end(unit, stage):
+        for group in range(3):
+            stage_copy(unit, group, stage).wait()
+            half, own, other, bit = span(unit, group, stage)
+            keep[unit % SLOTS, group, pl.ds(own, half)] += stage_in[stage][unit, group]
+            if stage + 1 < stages:
+                stage_copy(unit, group, stage + 1).start()
+            else:
+                final_copy(unit, group).start()
+
+    def final_wait(unit):
+        for group in range(3):
+            final_copy(unit, group).wait()
+
+    def tick(number):
+        for stage in reversed(range(stages)):
+            unit = number - stage
+            if 0 <= unit < 12:
+                stage_end(unit, stage)
+
+    def make_unit(unit, lhs_half, rhs):
+        if unit >= SLOTS:
+            final_wait(unit - SLOTS)
+        kept, sent = unit % SLOTS, SLOTS + unit % 2
+        index = [kept + core * (sent - kept), sent + core * (kept - sent)]
+        half_blocks = wide // 2
+        for half in range(2):
+            product = dot(lhs_half(half), rhs())
+            for row_block in range(half_blocks):
+                for group in range(3):
+                    top = row_block * block_rows + group * group_rows
+                    for column_block in range(narrow):
+                        where = place(unit, group, half * half_blocks + row_block, column_block)
+                        keep[index[row_block % 2], group, where] = product[
+                            top : top + group_rows,
+                            column_block * width : (column_block + 1) * width,
+                        ]
+        core_start(unit)
+
+    def load(src, dst, number):
+        copy = pltpu.make_async_copy(src, dst, load_sem.at[number])
+        copy.start()
+        return copy
+
+    tok_load = load(tokens_in, tok, 0)
+    qkv_load = load(qkv_in, w_a.at[:, pl.ds(0, 3 * model)], 1)
+    proj_load = load(proj_in, w_p, 2)
+    cot_load = load(cotangent_in, cot, 3)
+    down_load = load(down_in, w_b, 4)
+    vec[...] = jnp.zeros_like(vec)
+    qkv_bias[:, 0:model] = query_bias[...]
+    qkv_bias[:, model : 2 * model] = jnp.zeros((1, model), F32)
+    qkv_bias[:, 2 * model :] = value_bias[...]
+
+    def field_rows(field):
+        return pl.ds(pl.multiple_of(field * patches, patches), patches)
+
+    def each_field(step):
+        def body(field, carry):
+            step(field)
+            return carry
+
+        lax.fori_loop(0, fields, body, 0)
+
+    tok_load.wait()
+
+    def norm_one(field):
+        rows = field_rows(field)
+        unit_rows, scale = standardise(tok[rows, :].astype(F32))
+        n1[rows, :] = (unit_rows * gain_one[...] + shift_one[...]).astype(BF16)
+
+    each_field(norm_one)
+    qkv_load.wait()
+
+    def project(tile, carry):
+        columns = pl.ds(pl.multiple_of(tile * 256, 256), 256)
+        qkv[:, columns] = (dot(n1[...], w_a[:, columns]) + qkv_bias[:, columns]).astype(BF16)
+        return carry
+
+    lax.fori_loop(0, 3 * model // 256, project, 0)
+    up_load = load(up_in, w_a, 5)
+
+    lane = lax.broadcasted_iota(jnp.int32, (1, 128), 1)
+    head_masks = [(lane < 64).astype(BF16), (lane >= 64).astype(BF16)]
+    lane_full = lax.broadcasted_iota(jnp.int32, (patches, 128), 1)
+    pairs = model // 128
+
+    def stack_heads(rows, factor=1.0):
+        return jnp.concatenate([rows * (mask * BF16(factor)) for mask in head_masks], 0)
+
+    def pick_heads(rows):
+        return jnp.where(lane_full < 64, rows[:patches], rows[patches:])
+
+    def soften(stacked, key_rows, visible):
+        scores = jnp.where(visible, dot_nt(stacked, key_rows), -1e30)
+        exponent = jnp.exp(scores - jnp.max(scores, -1, keepdims=True))
+        return exponent * (1.0 / jnp.sum(exponent, -1, keepdims=True))
+
+    def pair_columns(pair):
+        return [pl.ds(part * model + pair * 128, 128) for part in range(3)]
+
+    def visible_of(field):
+        return jnp.broadcast_to(land[pl.ds(field, 1), :], (2 * patches, patches)) > 0
+
+    def attend(field):
+        rows = field_rows(field)
+        visible = visible_of(field)
+        for pair in range(pairs):
+            at_q, at_k, at_v = pair_columns(pair)
+            attention = soften(stack_heads(qkv[rows, at_q], 0.125), qkv[rows, at_k], visible)
+            both = dot(attention.astype(BF16), qkv[rows, at_v])
+            att[rows, pl.ds(pair * 128, 128)] = pick_heads(both).astype(BF16)
+
+    each_field(attend)
+    proj_load.wait()
+
+    def residual(tile, carry):
+        columns = pl.ds(pl.multiple_of(tile * 256, 256), 256)
+        mid[:, columns] = (
+            tok[:, columns].astype(F32) + dot(att[...], w_p[:, columns]) + proj_bias[:, columns]
+        )
+        return carry
+
+    lax.fori_loop(0, model // 256, residual, 0)
+
+    def norm_two(field):
+        rows = field_rows(field)
+        unit_rows, scale = standardise(mid[rows, :])
+        normed = (unit_rows * gain_two[...] + shift_two[...]).astype(BF16)
+        n2[rows, :] = normed
+        left[:, rows] = normed.T
+
+    each_field(norm_two)
+
+    root = 0.7978845608028654
+
+    def hidden_columns(part, column_block):
+        return column_block * (hidden_width // narrow) + part * chunk
+
+    def feed(part):
+        for column_block in range(narrow):
+            first = hidden_columns(part, column_block)
+            columns = pl.ds(first, chunk)
+            here = pl.ds(column_block * chunk, chunk)
+            hidden = dot(n2[...], w_a[:, columns]) + up_bias[:, columns]
+            pulled = dot_nt(cot[...], w_b[columns, :])
+            square = hidden * hidden
+            bent = jnp.tanh(hidden * (root + (root * 0.044715) * square))
+            cdf = 0.5 + 0.5 * bent
+            activated = (hidden * cdf).astype(BF16)
+            slope = cdf + (hidden * (0.5 - 0.5 * bent * bent)) * (
+                root + (3 * root * 0.044715) * square
+            )
+            grad = (pulled * slope).astype(BF16)
+            act[:, here] = activated
+            hgr[:, here] = grad
+            act_t[columns, :] = activated.T
+            vec[pl.ds(3 + first // model, 1), pl.ds(first % model, chunk)] = column_sums(
+                grad.astype(F32)
+            )
+
+    def feed_sums(part):
+        for column_block in range(narrow):
+            columns = pl.ds(hidden_columns(part, column_block), chunk)
+            here = pl.ds(column_block * chunk, chunk)
+            for target, term in (
+                (acc, lambda: dot(act[:, here], w_b[columns, :])),
+                (ngr, lambda: dot_nt(hgr[:, here], w_a[:, columns])),
+            ):
+                if part == 0 and column_block == 0:
+                    target[...] = term()
+                else:
+                    target[...] += term()
+
+    def left_half(half):
+        return left[pl.ds(half * (model // 2), model // 2), :]
+
+    def up_unit(part):
+        make_unit(part, left_half, lambda: hgr[...])
+
+    def down_unit(part):
+        def rows(half):
+            return jnp.concatenate(
+                [
+                    act_t[pl.ds(block * 4 * block_rows + part * block_rows, block_rows), :]
+                    for block in range(half * wide // 2, (half + 1) * wide // 2)
+                ],
+                0,
+            )
+
+        make_unit(4 + part, rows, lambda: cot[...])
+
+    def store_output(field):
+        rows = field_rows(field)
+        act[rows, :] = (mid[rows, :] + acc[rows, :] + down_bias[...]).astype(BF16)
+
+    output_copy = pltpu.make_async_copy(act, output_out, store_sem.at[0])
+    tokens_copy = pltpu.make_async_copy(acc, tokens_out, store_sem.at[1])
+
+    def add_sums(row, columns, rows):
+        vec[pl.ds(row, 1), columns] += column_sums(rows)
+
+    everything = pl.ds(0, model)
+
+    def middle_back(field):
+        rows = field_rows(field)
+        unit_rows, scale = standardise(mid[rows, :])
+        grads = ngr[rows, :]
+        top = cot[rows, :].astype(F32)
+        add_sums(7, everything, top)
+        add_sums(10, everything, grads * unit_rows)
+        add_sums(11, everything, grads)
+        total = top + norm_back(unit_rows, scale, grads * gain_two[...])
+        acc[rows, :] = total
+        low = total.astype(BF16)
+        hgr[rows, :] = low
+        add_sums(2, everything, low.astype(F32))
+
+    def attend_back(field):
+        rows = field_rows(field)
+        visible = visible_of(field)
+        for pair in range(pairs):
+            at_q, at_k, at_v = pair_columns(pair)
+            key_rows, values = qkv[rows, at_k], qkv[rows, at_v]
+            stacked = stack_heads(qkv[rows, at_q], 0.125)
+            attention = soften(stacked, key_rows, visible)
+            pulled = stack_heads(act[rows, pl.ds(pair * 128, 128)])
+            values_grad = dot_tn(attention.astype(BF16), pulled).astype(BF16)
+            inner = dot_nt(pulled, values)
+            inner = inner - jnp.sum(attention * inner, -1, keepdims=True)
+            scores_grad = (attention * inner).astype(BF16)
+            queries_grad = (pick_heads(dot(scores_grad, key_rows)) * 0.125).astype(BF16)
+            keys_grad = dot_tn(scores_grad, stacked).astype(BF16)
+            qkv[rows, at_q] = queries_grad
+            qkv[rows, at_k] = keys_grad
+            qkv[rows, at_v] = values_grad
+            here = pl.ds(pair * 128, 128)
+            add_sums(0, here, queries_grad.astype(F32))
+            add_sums(1, here, values_grad.astype(F32))
+
+    def proj_unit():
+        for field in range(fields):
+            left[:, field_rows(field)] = att[field_rows(field), :].T
+        make_unit(8, left_half, lambda: hgr[...])
+
+    def qkv_unit(part):
+        if part == 0:
+            for field in range(fields):
+                left[:, field_rows(field)] = n1[field_rows(field), :].T
+        stride = 3 * model // narrow
+        make_unit(
+            9 + part,
+            left_half,
+            lambda: jnp.concatenate(
+                [
+                    qkv[:, pl.ds(block * stride + part * width, width)]
+                    for block in range(narrow)
+                ],
+                1,
+            ),
+        )
+
+    def source_back(field):
+        rows = field_rows(field)
+        unit_rows, scale = standardise(tok[rows, :].astype(F32))
+        grads = ngr[rows, :]
+        add_sums(8, everything, grads * unit_rows)
+        add_sums(9, everything, grads)
+        acc[rows, :] += norm_back(unit_rows, scale, grads * gain_one[...])
+
+    def vec_copy(number):
+        return remote(
+            vec, vec_in.at[number], vec_send.at[number], vec_recv.at[number], all_bits[number]
+        )
+
+    def vec_end(number):
+        vec_copy(number).wait()
+        vec[...] += vec_in[number]
+        if number + 1 < len(all_bits):
+            vec_copy(number + 1).start()
+
+    up_load.wait()
+    down_load.wait()
+    cot_load.wait()
+    feed(0)
+    pl.semaphore_wait(barrier, len(all_bits))
+    up_unit(0)
+    feed_sums(0)
+    core_end(0)
+    feed(1)
+    up_unit(1)
+    feed_sums(1)
+    core_end(1)
+
+    feed(2)
+    up_unit(2)
+    feed_sums(2)
+    tick(0)
+    core_end(2)
+
+    feed(3)
+    up_unit(3)
+    feed_sums(3)
+    tick(1)
+    core_end(3)
+
+    qkv_again = load(qkv_in, w_a.at[:, pl.ds(0, 3 * model)], 1)
+    down_unit(0)
+    each_field(store_output)
+    output_copy.start()
+    each_field(middle_back)
+    tick(2)
+    core_end(4)
+
+    down_unit(1)
+    output_copy.wait()
+    act[...] = dot_nt(hgr[...], w_p[...]).astype(BF16)
+    attend_back(0)
+    tick(3)
+    core_end(5)
+
+    down_unit(2)
+    lax.fori_loop(1, fields - 1, lambda field, carry: (attend_back(field), carry)[1], 0)
+    tick(4)
+    core_end(6)
+
+    down_unit(3)
+    attend_back(fields - 1)
+    tick(5)
+    core_end(7)
+
+    proj_unit()
+    tick(6)
+    core_end(8)
+
+    qkv_unit(0)
+    qkv_again.wait()
+    ngr[...] = dot_nt(qkv[...], w_a[:, pl.ds(0, 3 * model)])
+    tick(7)
+    core_end(9)
+
+    qkv_unit(1)
+    each_field(source_back)
+    tokens_copy.start()
+    vec_copy(0).start()
+    tick(8)
+    core_end(10)
+
+    qkv_unit(2)
+    tick(9)
+    core_end(11)
+
+    left_over = list(range(len(all_bits)))
+    for number in range(10, 12 + stages):
+        if left_over:
+            vec_end(left_over.pop(0))
+        tick(number)
+    while left_over:
+        vec_end(left_over.pop(0))
+    vec_store = pltpu.make_async_copy(vec, vec_out, store_sem.at[2])
+    vec_store.start()
+    tokens_copy.wait()
+    for unit in range(12 - SLOTS, 12):
+        final_wait(unit)
+    vec_store.wait()
+
+
+def local_fused(wide, narrow, *args):
+    (
+        tokens, land_mask, cotangent, qkv_weight, query_bias, value_bias, proj_weight, proj_bias,
+        up_weight, up_bias, down_weight, down_bias, norm1_gain, norm1_shift, norm2_gain, norm2_shift,
+    ) = args
+    fields, patches, model = tokens.shape
+    rows = fields * patches
+    hidden_width = up_weight.shape[1]
+    width, block_rows = model // narrow, model // wide
+    bits = (wide * narrow).bit_length() - 1
+    blocks = wide * narrow // 2
+    group_rows = block_rows // 3
+    anywhere = pl.BlockSpec(memory_space=pl.ANY)
+    in_vmem = pl.BlockSpec(memory_space=pltpu.VMEM)
+
+    def vmem(shape, dtype=F32):
+        return pltpu.VMEM(shape, dtype)
+
+    dma = pltpu.SemaphoreType.DMA
+    results = pl.pallas_call(
+        lambda *refs: layer_kernel(wide, narrow, fields, patches, *refs),
+        out_shape=[
+            jax.ShapeDtypeStruct((rows, model), BF16),
+            jax.ShapeDtypeStruct((rows, model), F32),
+            jax.ShapeDtypeStruct((block_rows, 3 * width), F32),
+            jax.ShapeDtypeStruct((block_rows, width), F32),
+            jax.ShapeDtypeStruct((block_rows, 4 * width), F32),
+            jax.ShapeDtypeStruct((4 * block_rows, width), F32),
+            jax.ShapeDtypeStruct((16, model), F32),
+        ],
+        in_specs=[anywhere] * 6 + [in_vmem] * 10,
+        out_specs=[anywhere] * 7,
+        scratch_shapes=[
+            vmem((rows, model), BF16),
+            vmem((rows, model), BF16),
+            vmem((rows, model), BF16),
+            vmem((rows, 3 * model), BF16),
+            vmem((rows, model), BF16),
+            vmem((rows, model)),
+            vmem((rows, model), BF16),
+            vmem((hidden_width, rows), BF16),
+            vmem((rows, model), BF16),
+            vmem((rows, model), BF16),
+            vmem((rows, model)),
+            vmem((rows, model)),
+            vmem((model, rows), BF16),
+            vmem((model, hidden_width), BF16),
+            vmem((hidden_width, model), BF16),
+            vmem((model, model), BF16),
+            vmem((1, 3 * model)),
+            vmem((SLOTS + 2, 3, blocks, group_rows, width)),
+            vmem((2, 3, blocks, group_rows, width)),
+            *[vmem((12, 3, blocks >> (s + 1), group_rows, width)) for s in range(4)],
+            vmem((16, model)),
+            vmem((bits, 16, model)),
+            dma((6,)),
+            dma((2,)),
+            dma((2,)),
+            pltpu.SemaphoreType.REGULAR,
+            dma((12, bits - 1, 3)),
+            dma((12, bits - 1, 3)),
+            dma((SLOTS, 3)),
+            dma((bits,)),
+            dma((bits,)),
+            dma((3,)),
+        ],
+        compiler_params=pltpu.CompilerParams(
+            collective_id=0, has_side_effects=True, vmem_limit_bytes=63 << 20
+        ),
+        name="encoder_layer",
+    )(
+        tokens.reshape(rows, model),
+        cotangent.reshape(rows, model),
+        qkv_weight,
+        proj_weight,
+        up_weight,
+        down_weight,
+        land_mask,
+        query_bias.reshape(1, -1),
+        value_bias.reshape(1, -1),
+        proj_bias.reshape(1, -1),
+        up_bias.reshape(1, -1),
+        down_bias.reshape(1, -1),
+        norm1_gain.reshape(1, -1),
+        norm1_shift.reshape(1, -1),
+        norm2_gain.reshape(1, -1),
+        norm2_shift.reshape(1, -1),
+    )
+    output, tokens_grad, qkv_grad, proj_grad, up_grad, down_grad, vectors = results
+    return (
+        output.reshape(tokens.shape),
+        tokens_grad.reshape(tokens.shape),
+        qkv_grad,
+        vectors[0],
+        vectors[1],
+        proj_grad,
+        vectors[2],
+        up_grad,
+        vectors[3:7].reshape(-1),
+        down_grad,
+        vectors[7],
+        vectors[8],
+        vectors[9],
+        vectors[10],
+        vectors[11],
+    )
 
 
 def layer_norm(inputs, norm_gain, norm_shift):
@@ -194,6 +835,7 @@
 
 
 def solution(mesh):
+    wide, narrow = mesh.shape["wide"], mesh.shape["narrow"]
     placed = (
         P(("wide", "narrow"), None, None),
         P(("wide", "narrow"), None),
@@ -212,8 +854,13 @@
         P(),
         P(),
     )
+    fused = (wide, narrow) == (16, 2)
+
+    def layer(*args):
+        return local_fused(wide, narrow, *args) if fused else local(*args)
+
     return jax.shard_map(
-        local,
+        layer,
         mesh=mesh,
         in_specs=placed,
         out_specs=(

time: 522 us -> 158 us (0.30); the launches traced: 514 us -> 157 us
  waiting for transfers between devices: 333 us -> 0 us
  Pallas kernels: 0 us -> 136 us
  matrix products: 80.8 us -> 0 us
  blocking collectives: 42 us -> 0 us
  other arithmetic: 17.4 us -> 0 us
  between operations: 15.1 us -> 0.7 us
    reduce_scatter x8 -> x0, waiting for transfers between devices: 333 us -> none  [the longest x2 203 us: share_sums(): lax.psum_scatter(former, 'wide', scatter_dimension=0, tiled=True)]
    pallas_call x0 -> x1, Pallas kernels: none -> 136 us  [local_fused(): pl.pallas_call(lambda *refs: layer_kernel(wide, narrow, fields, patches,...]
    dot_general x18 -> x0, matrix products: 80.8 us -> none  [the longest x1 10.3 us: local(): jnp.einsum('fpn,fpd->nd', activated, cotangent, preferred_element_type=jn...]
    psum x1 -> x0, blocking collectives: 42 us -> none  [local(): lax.psum((query_bias_local, value_bias_local, proj_bias_local, up_bias_lo...]
    reduce_sum x9 -> x0, other arithmetic: 13.6 us -> none  [the longest x1 2.78 us: local(): joint_sums = jnp.sum(joint_grad.astype(jnp.float32), axis=(0, 1))]
    convert_element_type x3 -> x0, local copies, waits for them, and re-layouts: 6.87 us -> none  [the longest x1 2.3 us: local(): (joint[..., 2 * model_width:] + value_bias).astype(jnp.bfloat16)]
    reshape x3 -> x9, local copies, waits for them, and re-layouts: 6.94 us -> 10.7 us  [the longest x1 1.27 us: local_fused(): query_bias.reshape(1, -1)]
  transfers between devices with their start and end apart: 8 -> 0, of which waited for: 5 -> 0; matrix products, arithmetic and copies ran while one was open for 15% -> 0% of each run, Pallas kernels for 0% -> 0%
where the time goes in v1:
time: 158 us; the launch traced here: 157 us
  Pallas kernels  136 us (86%)
  local copies, waits for them, and re-layouts  20.6 us (13%)
    pallas_call x1, Pallas kernels, local_fused(): pl.pallas_call(lambda *refs: layer_kernel(wide, narrow, fields, patches,...  136 us
    unnamed x14, local copies, waits for them, and re-layouts  7.52 us

profile of v1, /device:TPU:0, one launch (start us, length us, event | category | flops | bytes accessed | tf_op | source)
XLA Modules:
  0.0 157.4 jit_solution(3614920109540056940)
XLA Ops:
  0.6 1.3 reshape.74.refs_7_
  1.9 1.3 reshape.75.refs_8_
  3.2 1.3 reshape.76.refs_9_
  4.4 1.3 reshape.78.refs_11_
  5.7 1.3 reshape.79.refs_12_
  7.0 1.3 reshape.80.refs_13_
  8.2 1.3 reshape.81.refs_14_
  9.5 1.3 reshape.82.refs_15_
  10.8 136.1 %encoder_layer.1 = (bf16[512,768]{1,0:T(8,128)(2,1)}, f32[512,768]{1,0:T(8,128)}, f32[48,1152]{1,0:T(8,128)}, f32[48,384]{1,0:T(8,128)}, f32[48,1536]{1,0:T(8,12...) custom-call(bf16[512,768]{1,0:T(8,128)(2,1)} %bitcast.6, bf16[512,768]{1,0:T(8,128)(2,1)} %bitcast.7, ...), custom_call_target="tpu_custom_call" | custom-call | tf_op jit(solution)/shard_map/encoder_layer/pallas_call | solution.py:561
  146.9 0.0 copy-start.2
  146.9 0.0 copy-start.3
  146.9 0.0 copy-start.1
  146.9 0.0 copy-start
  146.9 1.6 %slice_reduce_fusion = (f32[768]{0:T(1024)}, f32[768]{0:T(1024)}, f32[768]{0:T(1024)}, f32[768]{0:T(1024)}, f32[768]{0:T(1024)}, /*index=5*/f32[768]{0:T(1024)}, f32[768]{0:T(1024)}, f32[768]{0:T(1024)}) fusion(f32[16,768]{1,0:T(8,128)} %get-tuple-element.25), kind=kLoop, calls=%fused_computation | loop fusion | bytes 49152 | tf_op jit(solution)/shard_map/slice | solution.py:646
  148.5 0.7 slice.30
  149.3 0.6 reshape.85
  149.9 2.1 %copy.37 = bf16[4,128,768]{2,1,0:T(8,128)(2,1)} copy(bf16[4,128,768]{2,1,0:T(8,128)(2,1)} %bitcast.8) | data formatting | bytes 1572864
  151.9 2.7 %copy.38 = f32[4,128,768]{2,1,0:T(8,128)} copy(f32[4,128,768]{2,1,0:T(8,128)} %bitcast.5) | data formatting | bytes 3145728
  154.6 0.0 copy-done.2
  154.6 0.7 copy.39
  155.3 0.0 copy-done.3
  155.3 0.6 copy.40
  155.9 0.0 copy-done.1
  155.9 0.7 copy.41
  156.7 0.0 copy-done
  156.7 0.7 copy.42
Async XLA Ops:
  146.9 7.8 %copy-start.2 = (f32[48,1152]{1,0:T(8,128)S(1)}, f32[48,1152]{1,0:T(8,128)}, u32[]{:S(2)}) copy-start(f32[48,1152]{1,0:T(8,128)} %get-tuple-element.54) | copy-start | bytes 663556
  146.9 8.4 %copy-start.3 = (f32[48,384]{1,0:T(8,128)S(1)}, f32[48,384]{1,0:T(8,128)}, u32[]{:S(2)}) copy-start(f32[48,384]{1,0:T(8,128)} %get-tuple-element.57) | copy-start | bytes 221188
  146.9 9.1 %copy-start.1 = (f32[48,1536]{1,0:T(8,128)S(1)}, f32[48,1536]{1,0:T(8,128)}, u32[]{:S(2)}) copy-start(f32[48,1536]{1,0:T(8,128)} %get-tuple-element.59) | copy-start | bytes 884740
  146.9 9.8 %copy-start = (f32[192,384]{1,0:T(8,128)S(1)}, f32[192,384]{1,0:T(8,128)}, u32[]{:S(2)}) copy-start(f32[192,384]{1,0:T(8,128)} %get-tuple-element.61) | copy-start | bytes 884740
